TPU v7x, 512 devices: a whole 4x8x8 slice. The times are simulated.
512 devices in a mesh: row: 16 (over z, y_hi), col: 32 (over y_lo, x, core).
Axes of the slice: x: 4, y: 8 (y_hi: 2, y_lo: 4; y = y_hi * 4 + y_lo), z: 8, core: 2. Of those that a mesh axis runs over, the one named last changes fastest.
Arguments:
- weight_half: bfloat16 [8192, 14336], P('row', 'col'), may hold values from -3 to 3
- weight_full: float32 [8192, 14336], P('row', 'col'), may hold values from -3 to 3
- adapter_b: float32 [2, 8192, 128], P(None, ('row', 'col')), may hold values from -6 to 6
- adapter_a: float32 [2, 128, 14336], P(None, None, ('col', 'row')), may hold values from -1 to 1
- moments_b: float32 [2, 2, 8192, 128], P(None, None, ('row', 'col')), may hold values from 0.01 to 1
- moments_a: float32 [2, 2, 128, 14336], P(None, None, None, ('col', 'row')), may hold values from 0.01 to 1
- reset_rows: int32 [2, 64], replicated, may hold values 0 or 1
- reset_cols: int32 [2, 112], replicated, may hold values 0 or 1
Outputs:
- merged_half: bfloat16 [8192, 14336], P('row', 'col')
- merged_full: float32 [8192, 14336], P('row', 'col')
- restart_b: float32 [2, 2, 8192, 128], P(None, None, ('row', 'col'))
- restart_a: float32 [2, 2, 128, 14336], P(None, None, None, ('col', 'row'))
All inputs are finite; a program needn't handle non-finite values.
Results may differ from a plain program's by a relative error of at most 0.001.
Values sent between devices are 32-bit elements; how exact they have to be, the bound alone decides.
A program may use at most 64 MiB of HBM per device.

v0:
```python
import jax
import jax.numpy as jnp
from jax import lax
from jax.sharding import PartitionSpec as P

LAYERS = 2
BLOCK = 128


merge_scale = 0.25


def per_device(
    weight_half, weight_full, adapter_b, adapter_a, moments_b, moments_a, reset_rows, reset_cols
):
    row_count = lax.axis_size("row")
    col_count = lax.axis_size("col")
    row_pos = lax.axis_index("row")
    col_pos = lax.axis_index("col")
    rows_owned = adapter_b.shape[1]
    cols_owned = adapter_a.shape[2]
    row_first = (row_pos * col_count + col_pos) * rows_owned
    col_first = (col_pos * row_count + row_pos) * cols_owned
    updates = []
    for layer_index in range(LAYERS):
        cols_block = lax.all_gather(adapter_a[layer_index], "row", axis=1, tiled=True)

        def product(segment, offset, cols_block=cols_block):
            return jnp.dot(
                segment,
                cols_block,
                precision=lax.Precision.HIGHEST,
                preferred_element_type=jnp.float32,
            )

        updates.append(
            merge_scale
            * product(
                lax.all_gather(adapter_b[layer_index], "col", axis=0, tiled=True), jnp.int32(0)
            )
        )
    merged_half = (weight_half.astype(jnp.float32) + updates[0]).astype(jnp.bfloat16)
    merged_full = weight_full + updates[1]
    row_flags = lax.dynamic_slice_in_dim(
        jnp.repeat(reset_rows, BLOCK, axis=1), row_first, rows_owned, 1
    )
    col_flags = lax.dynamic_slice_in_dim(
        jnp.repeat(reset_cols, BLOCK, axis=1), col_first, cols_owned, 1
    )
    restart_b = jnp.where(row_flags[:, None, :, None] == 1, jnp.zeros_like(moments_b), moments_b)
    restart_a = jnp.where(col_flags[:, None, None, :] == 1, jnp.zeros_like(moments_a), moments_a)
    return (merged_half, merged_full, restart_b, restart_a)


def solution(mesh):
    return jax.shard_map(
        per_device,
        mesh=mesh,
        in_specs=(
            P("row", "col"),
            P("row", "col"),
            P(None, ("row", "col"), None),
            P(None, None, ("col", "row")),
            P(None, None, ("row", "col"), None),
            P(None, None, None, ("col", "row")),
            P(),
            P(),
        ),
        out_specs=(
            P("row", "col"),
            P("row", "col"),
            P(None, None, ("row", "col"), None),
            P(None, None, None, ("col", "row")),
        ),
        check_vma=False,
    )
```

profile of v0, /device:TPU:1, one launch (start us, length us, event | category | flops | bytes accessed | tf_op | source)
XLA Modules:
  0.0 199.1 jit_solution(6638508533006047097)
XLA Ops:
  0.6 0.0 copy-start
  0.6 0.0 copy-start.2
  0.7 0.8 fusion.5
  1.5 54.9 %all-gather.1 = f32[1,128,448]{1,0,2:T(1,128)S(1)} all-gather(f32[1,128,28]{1,0,2:T(1,128)S(1)} %get-tuple-element.5), channel_id=3, replica_groups=mesh['row'=16,'col'=32] {'row'}, dimensions={2}, use_global_device_ids=true | all-gather | bytes 243712 | tf_op jit(solution)/shard_map/all_gather | solution.py:26
  56.5 0.7 fusion.6
  57.2 49.3 %all-gather = f32[1,512,128]{2,1,0:T(8,128)S(1)} all-gather(f32[1,16,128]{2,1,0:T(8,128)S(1)} %get-tuple-element.7), channel_id=2, replica_groups=mesh['row'=16,'col'=32] {'col'}, dimensions={1}, use_global_device_ids=true | all-gather | bytes 270336 | tf_op jit(solution)/shard_map/all_gather | solution.py:39
  106.4 0.0 copy-done.2
  106.4 0.0 copy-start.1
  106.4 1.7 fusion.2
  108.1 40.9 %all-gather.3 = f32[1,128,448]{1,0,2:T(1,128)S(1)} all-gather(f32[1,128,28]{1,0,2:T(1,128)S(1)} %get-tuple-element.4), channel_id=5, replica_groups=mesh['row'=16,'col'=32] {'row'}, dimensions={2}, use_global_device_ids=true | all-gather | bytes 243712 | tf_op jit(solution)/shard_map/all_gather | solution.py:26
  149.1 44.9 %all-gather.2 = f32[1,512,128]{2,1,0:T(8,128)S(1)} all-gather(f32[1,16,128]{2,1,0:T(8,128)S(1)} %get-tuple-element.6), channel_id=4, replica_groups=mesh['row'=16,'col'=32] {'col'}, dimensions={1}, use_global_device_ids=true | all-gather | bytes 270336 | tf_op jit(solution)/shard_map/all_gather | solution.py:39
  194.0 0.0 copy-done.1
  194.0 0.0 copy-start.5
  194.0 1.9 fusion
  195.9 0.0 copy-done.5
  195.9 0.1 broadcast_bitcast_fusion.1
  195.9 0.0 copy-start.4
  195.9 0.1 copy.17
  196.0 0.1 dynamic-slice_compare_fusion.1
  196.1 0.6 copy-done.4
  196.7 0.7 broadcast_select_fusion.1
  197.4 0.0 copy-done
  197.4 0.1 broadcast_bitcast_fusion
  197.5 0.0 copy-start.3
  197.5 0.1 copy.16
  197.6 0.1 dynamic-slice_compare_fusion
  197.6 0.7 copy-done.3
  198.3 0.7 broadcast_select_fusion
Async XLA Ops:
  0.6 196.8 %copy-start = (s32[2,112]{1,0:T(2,128)S(1)}, s32[2,112]{1,0:T(2,128)}, u32[]{:S(2)}) copy-start(s32[2,112]{1,0:T(2,128)} %param.15) | copy-start | bytes 2692
  0.6 105.8 %copy-start.2 = (bf16[512,448]{0,1:T(8,128)(2,1)S(1)}, bf16[512,448]{0,1:T(8,128)(2,1)}, u32[]{:S(2)}) copy-start(bf16[512,448]{0,1:T(8,128)(2,1)} %param.8) | copy-start | bytes 1376260
  106.4 87.6 %copy-start.1 = (f32[512,448]{0,1:T(8,128)S(1)}, f32[512,448]{0,1:T(8,128)}, u32[]{:S(2)}) copy-start(f32[512,448]{0,1:T(8,128)} %param.9) | copy-start | bytes 2752516
  194.0 1.9 copy-start.5
  195.9 0.8 copy-start.4
  197.5 0.8 copy-start.3
where the time goes:
time: 199 us
  blocking collectives  190 us (95%)
  matrix products  3.55 us (2%)
  local copies, waits for them, and re-layouts  3.13 us (2%)
    all_gather x2, blocking collectives, per_device(): lax.all_gather(adapter_a[layer_index], 'row', axis=1, tiled=True)  95.9 us
    all_gather x2, blocking collectives, per_device(): lax.all_gather(adapter_b[layer_index], 'col', axis=0, tiled=True)  94.2 us

commit v1 on v0

v1 whole, which is shorter than its diff:
```python
import functools

import jax
import jax.numpy as jnp
from jax import lax
from jax.experimental import pallas as pl
from jax.experimental.pallas import tpu as pltpu
from jax.sharding import PartitionSpec as P

LAYERS = 2
BLOCK = 128
MERGE_SCALE = 0.25
MESH = pl.DeviceIdType.MESH
NZ, NH, NY, NX, NC = 8, 2, 4, 4, 2
REACH = {(1, 0): 4, (-1, 0): 3, (1, 1): 3, (-1, 1): 4}

A_PARTNER = 0
A_CHAIN = {}
for _key, _reach in REACH.items():
    for _d in range(1, _reach + 1):
        A_CHAIN[_key + (_d,)] = 1 + len(A_CHAIN)
B_LINE = {k: 1 + len(A_CHAIN) + k - 1 for k in range(1, NY)}
_next = 1 + len(A_CHAIN) + len(B_LINE)
B_NEAR = {1: _next, -1: _next + 1}
B_FAR = {1: _next + 2, -1: _next + 3}
B_CORE = {0: _next + 4, 1: _next + 5, -1: _next + 6, (2, 1): _next + 7, (2, -1): _next + 8}
MESSAGES = _next + 9


def gather_merge(
    wh_ref, wf_ref, b_ref, a_ref, mb_ref, ma_ref, rr_ref, rc_ref,
    oh_ref, of_ref, ob_ref, oa_ref,
    a_all, b_all, b_cat, row_flags, col_flags, send_sem, recv_sem, local_sem,
):
    row, col = lax.axis_index("row"), lax.axis_index("col")
    z, h = row // NH, row % NH
    y, x, core = col // (NX * NC), (col // NC) % NX, col % NC
    a_rows = a_ref.shape[0]
    b_rows = b_ref.shape[0]
    rows_owned = b_rows // LAYERS
    cols_owned = a_rows // LAYERS

    def dev(dz=0, flip_h=0, ky=0, dx=0, flip_core=0):
        tz = (z + dz + NZ) % NZ
        th = (h + flip_h) % NH
        ty = pair(y, ky)
        tx = (x + dx + NX) % NX
        tc = (core + flip_core) % NC
        return (tz * NH + th, (ty * NX + tx) * NC + tc)

    def pair(v, k):
        low, high = v % 2, v // 2
        return ((high + k // 2) % 2) * 2 + (low + k % 2) % 2

    def a_slot(dz, flip_h):
        pos = ((z + dz + NZ) % NZ) * NH + (h + flip_h) % NH
        return a_all.at[pl.ds(pl.multiple_of(pos * a_rows, 8), a_rows), :]

    def b_slot(dx, y_first, y_count, flip_core=0):
        pos = (((core + flip_core) % NC) * NX + (x + dx + NX) % NX) * NY + y_first
        return b_all.at[pl.ds(pl.multiple_of(pos * b_rows, 8), y_count * b_rows), :]

    local = [
        pltpu.make_async_copy(a_ref, a_slot(0, 0), local_sem.at[0]),
        pltpu.make_async_copy(b_ref, b_slot(0, y, 1), local_sem.at[1]),
        pltpu.make_async_copy(mb_ref, ob_ref, local_sem.at[2]),
        pltpu.make_async_copy(ma_ref, oa_ref, local_sem.at[3]),
        pltpu.make_async_copy(wh_ref, oh_ref, local_sem.at[4]),
        pltpu.make_async_copy(wf_ref, of_ref, local_sem.at[5]),
        pltpu.make_async_copy(rr_ref, row_flags, local_sem.at[6]),
        pltpu.make_async_copy(rc_ref, col_flags, local_sem.at[7]),
    ]
    for c in local:
        c.start()

    barrier = pltpu.get_barrier_semaphore()
    greeted = [dev(flip_h=1), dev(dz=1), dev(dz=-1)]
    greeted += [dev(ky=k) for k in range(1, NY)]
    greeted += [dev(dx=1), dev(dx=-1), dev(flip_core=1)]
    for other in greeted:
        pl.semaphore_signal(barrier, inc=1, device_id=other, device_id_type=MESH)
    pl.semaphore_wait(barrier, len(greeted))

    sent = []

    def send(src, dst, message, device):
        c = pltpu.make_async_remote_copy(
            src_ref=src, dst_ref=dst, send_sem=send_sem.at[message],
            recv_sem=recv_sem.at[message], device_id=device, device_id_type=MESH,
        )
        c.start()
        sent.append(c)

    def arrive(dst, message):
        pltpu.make_async_copy(dst, dst, recv_sem.at[message]).wait()

    def a_send(s, o, d):
        slot = a_slot(-s * (d - 1), o)
        src = a_ref if (d == 1 and o == 0) else slot
        send(src, slot, A_CHAIN[s, o, d], dev(dz=s))

    def a_arrive(s, o, d):
        arrive(a_slot(-s * d, o), A_CHAIN[s, o, d])
        if d < REACH[s, o]:
            a_send(s, o, d + 1)

    send(a_ref, a_slot(0, 0), A_PARTNER, dev(flip_h=1))
    a_send(1, 0, 1)
    a_send(-1, 0, 1)
    for k in range(1, NY):
        send(b_ref, b_slot(0, y, 1), B_LINE[k], dev(ky=k))

    row_first = (row * (NY * NX * NC) + col) * rows_owned
    col_first = (col * (NZ * NH) + row) * cols_owned
    for i in (2, 3, 6, 7):
        local[i].wait()
    column = col_first + lax.broadcasted_iota(jnp.int32, (a_rows, BLOCK), 0) // 2
    first_block = col_first // BLOCK
    last_block = (col_first + cols_owned - 1) // BLOCK
    for l in range(LAYERS):
        keep_b = 1 - row_flags[l, row_first // BLOCK]
        ob_ref[l] = jnp.where(jnp.full(ob_ref.shape[1:], keep_b) == 0, 0.0, ob_ref[l])
        flag = jnp.where(column // BLOCK == first_block, col_flags[l, first_block], col_flags[l, last_block])
        oa_ref[l] = jnp.where(flag == 1, 0.0, oa_ref[l])

    a_arrive(1, 0, 1)
    a_arrive(-1, 0, 1)
    local[0].wait()
    local[1].wait()
    for k in range(1, NY):
        arrive(b_slot(0, pair(y, k), 1), B_LINE[k])
    for s in (1, -1):
        send(b_slot(0, 0, NY), b_slot(0, 0, NY), B_NEAR[s], dev(dx=s))
    send(b_slot(0, 0, NY), b_slot(0, 0, NY), B_CORE[0], dev(flip_core=1))
    arrive(a_slot(0, 1), A_PARTNER)
    a_send(1, 1, 1)
    a_send(-1, 1, 1)
    a_arrive(1, 0, 2)
    a_arrive(-1, 0, 2)
    for s in (1, -1):
        arrive(b_slot(-s, 0, NY), B_NEAR[s])
        half = b_slot(-s, 0 if s == 1 else NY // 2, NY // 2)
        send(half, half, B_FAR[s], dev(dx=s))
        send(b_slot(-s, 0, NY), b_slot(-s, 0, NY), B_CORE[-s], dev(flip_core=1))
    a_arrive(1, 1, 1)
    a_arrive(-1, 1, 1)
    a_arrive(1, 0, 3)
    a_arrive(-1, 0, 3)
    for s in (1, -1):
        half = b_slot(2, 0 if s == 1 else NY // 2, NY // 2)
        arrive(half, B_FAR[s])
        send(half, half, B_CORE[2, s], dev(flip_core=1))
    a_arrive(1, 1, 2)
    a_arrive(-1, 1, 2)
    for dx in (0, 1, -1):
        arrive(b_slot(dx, 0, NY, 1), B_CORE[dx])
    for s in (1, -1):
        arrive(b_slot(2, 0 if s == 1 else NY // 2, NY // 2, 1), B_CORE[2, s])

    def split(v):
        high = v.astype(jnp.bfloat16)
        return high, (v - high.astype(jnp.float32)).astype(jnp.bfloat16)

    for by in range(NY):
        for bx in range(NX):
            for bc in range(NC):
                at = ((bc * NX + bx) * NY + by) * b_rows
                to = ((by * NX + bx) * NC + bc) * rows_owned
                for l in range(LAYERS):
                    high, low = split(b_all[pl.ds(at + l * rows_owned, rows_owned), :])
                    b_cat[l, pl.ds(to, rows_owned), 0:128] = high
                    b_cat[l, pl.ds(to, rows_owned), 128:256] = high
                    b_cat[l, pl.ds(to, rows_owned), 256:384] = low

    a_arrive(1, 1, 3)
    a_arrive(-1, 1, 3)
    a_arrive(1, 0, 4)
    local[4].wait()
    local[5].wait()

    group = 2 * NH * cols_owned

    def merge(dj):
        j = (z // 2 + dj + NZ // 2) % (NZ // 2)
        first = pl.multiple_of(j * group, 16)
        for l, out in ((0, oh_ref), (1, of_ref)):
            high, low = split(a_all[pl.ds(first * 2 + l, group, stride=2), :])
            update = lax.dot_general(
                jnp.concatenate([high, low, high], axis=1), b_cat[l],
                (((1,), (1,)), ((), ())), preferred_element_type=jnp.float32,
            )
            at = (pl.ds(first, group), slice(None))
            out[at] = (out[at].astype(jnp.float32) + MERGE_SCALE * update).astype(out.dtype)

    merge(0)
    merge(1)
    merge(-1)
    a_arrive(-1, 1, 4)
    merge(2)
    for c in sent:
        c.wait_send()


def deliver(*refs):
    sems = refs[-1]
    half = (len(refs) - 1) // 2
    copies = [
        pltpu.make_async_copy(refs[i], refs[half + i], sems.at[i]) for i in range(half)
    ]
    for c in copies:
        c.start()
    for c in copies:
        c.wait()


def per_device(
    weight_half, weight_full, adapter_b, adapter_a, moments_b, moments_a, reset_rows, reset_cols
):
    layers, rows_owned, rank = adapter_b.shape
    cols_owned = adapter_a.shape[2]
    wh, wf = weight_half.T, weight_full.T
    b = adapter_b.reshape(layers * rows_owned, rank)
    a = adapter_a.transpose(2, 0, 1).reshape(cols_owned * layers, rank)
    mb = moments_b.reshape(layers, 2 * rows_owned, rank)
    ma = moments_a.transpose(0, 3, 1, 2).reshape(layers, cols_owned * 2, rank)
    shapes = [wh, wf, mb, ma]
    hbm = pl.BlockSpec(memory_space=pl.ANY)
    vmem = pl.BlockSpec(memory_space=pltpu.VMEM)
    merged = pl.pallas_call(
        gather_merge,
        name="gather_merge",
        out_shape=[pltpu.VMEM(s.shape, s.dtype) for s in shapes],
        in_specs=[hbm] * 8,
        out_specs=[vmem] * 4,
        scratch_shapes=[
            pltpu.VMEM((NZ * NH * a.shape[0], rank), jnp.float32),
            pltpu.VMEM((NY * NX * NC * b.shape[0], rank), jnp.float32),
            pltpu.VMEM((layers, NY * NX * NC * rows_owned, 3 * rank), jnp.bfloat16),
            pltpu.SMEM(reset_rows.shape, jnp.int32),
            pltpu.SMEM(reset_cols.shape, jnp.int32),
            pltpu.SemaphoreType.DMA((MESSAGES,)),
            pltpu.SemaphoreType.DMA((MESSAGES,)),
            pltpu.SemaphoreType.DMA((8,)),
        ],
        compiler_params=pltpu.CompilerParams(
            collective_id=0, has_side_effects=True, vmem_limit_bytes=32 * 1024 * 1024
        ),
    )(*(
        pltpu.with_memory_space_constraint(v, pltpu.HBM)
        for v in (wh, wf, b, a, mb, ma, reset_rows, reset_cols)
    ))
    merged = [pltpu.with_memory_space_constraint(m, pltpu.VMEM) for m in merged]
    oh, of, ob, oa = pl.pallas_call(
        deliver,
        name="deliver",
        out_shape=[jax.ShapeDtypeStruct(s.shape, s.dtype) for s in shapes],
        in_specs=[vmem] * 4,
        out_specs=[hbm] * 4,
        scratch_shapes=[pltpu.SemaphoreType.DMA((4,))],
    )(*merged)
    oa = oa.reshape(layers, cols_owned, 2, rank).transpose(0, 2, 3, 1)
    return oh.T, of.T, ob.reshape(moments_b.shape), oa


def solution(mesh):
    return jax.shard_map(
        per_device,
        mesh=mesh,
        in_specs=(
            P("row", "col"),
            P("row", "col"),
            P(None, ("row", "col"), None),
            P(None, None, ("col", "row")),
            P(None, None, ("row", "col"), None),
            P(None, None, None, ("col", "row")),
            P(),
            P(),
        ),
        out_specs=(
            P("row", "col"),
            P("row", "col"),
            P(None, None, ("row", "col"), None),
            P(None, None, None, ("col", "row")),
        ),
        check_vma=False,
    )
```

time: 199 us -> 34.4 us (0.17)
  the two profiles are of different devices: /device:TPU:1 before, /device:TPU:16 now
where the time goes in v1:
time: 34.4 us; the launch traced here: 34.3 us
  Pallas kernels  33.7 us (98%)
  between operations  0.64 us (2%)
    pallas_call x1, Pallas kernels, per_device(): pl.pallas_call(gather_merge, name='gather_merge', out_shape=[pltpu.VMEM(s...  32.5 us
    pallas_call x1, Pallas kernels, per_device(): pl.pallas_call(deliver, name='deliver', out_shape=[jax.ShapeDtypeStruct(s...  1.12 us

profile of v1, /device:TPU:16, one launch (start us, length us, event | category | flops | bytes accessed | tf_op | source)
XLA Modules:
  0.0 34.3 jit_solution(16246181666133161936)
XLA Ops:
  0.6 32.5 %gather_merge.1 = (bf16[448,512]{1,0:T(8,128)(2,1)S(1)}, f32[448,512]{1,0:T(8,128)S(1)}, f32[2,32,128]{2,1,0:T(8,128)S(1)}, f32[2,56,128]{2,1,0:T(8,128)S(1)}) custom-call(bf16[448,512]{1,0:T(8,128)(2,1)} %bitcast.17, f32[448,512]{1,0:T(8,128)} %bitcast.16, f32[32,128]{1,0:T(8,128)} %bitcast.21, f32[56,128]{1,0:T(8,128)} %bitcast.20, ...), custom_call_target="tpu_custom_call" | custom-call | tf_op jit(solution)/shard_map/gather_merge/pallas_call | solution.py:229
  33.2 1.1 %deliver.1 = (bf16[448,512]{1,0:T(8,128)(2,1)}, f32[448,512]{1,0:T(8,128)}, f32[2,32,128]{2,1,0:T(8,128)}, f32[2,56,128]{2,1,0:T(8,128)}) custom-call(bf16[448,512]{1,0:T(8,128)(2,1)S(1)} %get-tuple-element.12.refs_0_, f32[448,512]{1,0:T(8,128)S(1)} %get-tuple-element.13.refs_1_, f32[2,32,128]{2,1,0:T(8,128)S(1)} %get-tuple-element.14.refs_2_, ...), custom_call_target="tpu_custom_call" | custom-call | tf_op jit(solution)/shard_map/deliver/pallas_call | solution.py:253

commit v2 on v1

--- a/solution.py
+++ b/solution.py
@@ -12,25 +12,20 @@
 MERGE_SCALE = 0.25
 MESH = pl.DeviceIdType.MESH
 NZ, NH, NY, NX, NC = 8, 2, 4, 4, 2
-REACH = {(1, 0): 4, (-1, 0): 3, (1, 1): 3, (-1, 1): 4}
-
+X_STEPS = (2, 1, -1)
 A_PARTNER = 0
-A_CHAIN = {}
-for _key, _reach in REACH.items():
-    for _d in range(1, _reach + 1):
-        A_CHAIN[_key + (_d,)] = 1 + len(A_CHAIN)
-B_LINE = {k: 1 + len(A_CHAIN) + k - 1 for k in range(1, NY)}
-_next = 1 + len(A_CHAIN) + len(B_LINE)
-B_NEAR = {1: _next, -1: _next + 1}
-B_FAR = {1: _next + 2, -1: _next + 3}
-B_CORE = {0: _next + 4, 1: _next + 5, -1: _next + 6, (2, 1): _next + 7, (2, -1): _next + 8}
-MESSAGES = _next + 9
+A_Z = 1
+B_FIRST = A_Z + NH * NZ
+B_LINE = {k: B_FIRST + k for k in range(1, NY)}
+B_X = {d: B_FIRST + NY + i for i, d in enumerate(X_STEPS)}
+B_CORE = {d: B_FIRST + NY + len(X_STEPS) + i for i, d in enumerate((0, *X_STEPS))}
+MESSAGES = B_FIRST + NY + 2 * len(X_STEPS) + 1
 
 
 def gather_merge(
     wh_ref, wf_ref, b_ref, a_ref, mb_ref, ma_ref, rr_ref, rc_ref,
     oh_ref, of_ref, ob_ref, oa_ref,
-    a_all, b_all, b_cat, row_flags, col_flags, send_sem, recv_sem, local_sem,
+    a_all, b_all, b_cat, row_flags, col_flags, send_sem, recv_sem, local_sem, ready_sem,
 ):
     row, col = lax.axis_index("row"), lax.axis_index("col")
     z, h = row // NH, row % NH
@@ -52,16 +47,102 @@
         low, high = v % 2, v // 2
         return ((high + k // 2) % 2) * 2 + (low + k % 2) % 2
 
-    def a_slot(dz, flip_h):
-        pos = ((z + dz + NZ) % NZ) * NH + (h + flip_h) % NH
+    def at_z(t):
+        return (t * NH + h, col)
+
+    def a_slot(t, flip_h):
+        pos = t * NH + (h + flip_h) % NH
         return a_all.at[pl.ds(pl.multiple_of(pos * a_rows, 8), a_rows), :]
 
     def b_slot(dx, y_first, y_count, flip_core=0):
         pos = (((core + flip_core) % NC) * NX + (x + dx + NX) % NX) * NY + y_first
         return b_all.at[pl.ds(pl.multiple_of(pos * b_rows, 8), y_count * b_rows), :]
 
+    barrier = pltpu.get_barrier_semaphore()
+
+    def greet(other):
+        pl.semaphore_signal(barrier, inc=1, device_id=other, device_id_type=MESH)
+
+    def order_y(v):
+        return v + h * (NY - 1 - 2 * v)
+
+    def y_later(k):
+        return order_y(pair(y, k)) > order_y(y)
+
+    def x_later(d):
+        return (x + d + NX) % NX > x
+
+    def when(condition, action):
+        pl.when(condition)(action)
+
+    for t in range(1, NZ):
+        when(t > z, functools.partial(greet, at_z(t)))
+    when(h == 0, functools.partial(greet, dev(flip_h=1)))
+    for k in range(1, NY):
+        when(y_later(k), functools.partial(greet, dev(ky=k)))
+    for d in X_STEPS:
+        when(x_later(d), functools.partial(greet, dev(dx=d)))
+    when(core == 1, functools.partial(greet, dev(flip_core=1)))
+
+    def tell(number, other):
+        pl.semaphore_signal(ready_sem.at[number], inc=1, device_id=other, device_id_type=MESH)
+
+    def told(number):
+        pl.semaphore_wait(ready_sem.at[number], 1)
+
+    greetings = z + h + order_y(y) + x + 1 - core
+
+    @pl.when(greetings > 0)
+    def _():
+        pl.semaphore_wait(barrier, greetings)
+
+    def message(src, dst, number, device):
+        return pltpu.make_async_remote_copy(
+            src_ref=src, dst_ref=dst, send_sem=send_sem.at[number],
+            recv_sem=recv_sem.at[number], device_id=device, device_id_type=MESH,
+        )
+
+    def arrive(dst, number):
+        pltpu.make_async_copy(dst, dst, recv_sem.at[number]).wait()
+
+    def a_message(o, t):
+        slot = a_slot(z, o)
+        return message(slot if o else a_ref, slot, A_Z + o * NZ + (t - z + NZ) % NZ, at_z(t))
+
+    def a_arrive(o, t):
+        arrive(a_slot(t, o), A_Z + o * NZ + (z - t + NZ) % NZ)
+
+    partner = message(a_ref, a_slot(z, 0), A_PARTNER, dev(flip_h=1))
+    b_line = {k: message(b_ref, b_slot(0, y, 1), B_LINE[k], dev(ky=k)) for k in range(1, NY)}
+
+    @pl.when(h == 1)
+    def _():
+        partner.start()
+        tell(A_PARTNER, dev(flip_h=1))
+
+    for t in range(NZ - 1):
+        @pl.when(t < z)
+        def _():
+            a_message(0, t).start()
+            tell(A_Z + (t - z + NZ) % NZ, at_z(t))
+
+    for k, c in b_line.items():
+        @pl.when(jnp.logical_not(y_later(k)))
+        def _():
+            c.start()
+            tell(B_LINE[k], dev(ky=k))
+
+    for d in X_STEPS:
+        @pl.when(jnp.logical_not(x_later(d)))
+        def _():
+            tell(B_X[d], dev(dx=d))
+
+    @pl.when(core == 0)
+    def _():
+        tell(B_CORE[0], dev(flip_core=1))
+
     local = [
-        pltpu.make_async_copy(a_ref, a_slot(0, 0), local_sem.at[0]),
+        pltpu.make_async_copy(a_ref, a_slot(z, 0), local_sem.at[0]),
         pltpu.make_async_copy(b_ref, b_slot(0, y, 1), local_sem.at[1]),
         pltpu.make_async_copy(mb_ref, ob_ref, local_sem.at[2]),
         pltpu.make_async_copy(ma_ref, oa_ref, local_sem.at[3]),
@@ -72,43 +153,6 @@
     ]
     for c in local:
         c.start()
-
-    barrier = pltpu.get_barrier_semaphore()
-    greeted = [dev(flip_h=1), dev(dz=1), dev(dz=-1)]
-    greeted += [dev(ky=k) for k in range(1, NY)]
-    greeted += [dev(dx=1), dev(dx=-1), dev(flip_core=1)]
-    for other in greeted:
-        pl.semaphore_signal(barrier, inc=1, device_id=other, device_id_type=MESH)
-    pl.semaphore_wait(barrier, len(greeted))
-
-    sent = []
-
-    def send(src, dst, message, device):
-        c = pltpu.make_async_remote_copy(
-            src_ref=src, dst_ref=dst, send_sem=send_sem.at[message],
-            recv_sem=recv_sem.at[message], device_id=device, device_id_type=MESH,
-        )
-        c.start()
-        sent.append(c)
-
-    def arrive(dst, message):
-        pltpu.make_async_copy(dst, dst, recv_sem.at[message]).wait()
-
-    def a_send(s, o, d):
-        slot = a_slot(-s * (d - 1), o)
-        src = a_ref if (d == 1 and o == 0) else slot
-        send(src, slot, A_CHAIN[s, o, d], dev(dz=s))
-
-    def a_arrive(s, o, d):
-        arrive(a_slot(-s * d, o), A_CHAIN[s, o, d])
-        if d < REACH[s, o]:
-            a_send(s, o, d + 1)
-
-    send(a_ref, a_slot(0, 0), A_PARTNER, dev(flip_h=1))
-    a_send(1, 0, 1)
-    a_send(-1, 0, 1)
-    for k in range(1, NY):
-        send(b_ref, b_slot(0, y, 1), B_LINE[k], dev(ky=k))
 
     row_first = (row * (NY * NX * NC) + col) * rows_owned
     col_first = (col * (NZ * NH) + row) * cols_owned
@@ -123,39 +167,70 @@
         flag = jnp.where(column // BLOCK == first_block, col_flags[l, first_block], col_flags[l, last_block])
         oa_ref[l] = jnp.where(flag == 1, 0.0, oa_ref[l])
 
-    a_arrive(1, 0, 1)
-    a_arrive(-1, 0, 1)
+    @pl.when(h == 0)
+    def _():
+        told(A_PARTNER)
+        partner.start()
+
+    for k, c in b_line.items():
+        @pl.when(y_later(k))
+        def _():
+            told(B_LINE[k])
+            c.start()
+
     local[0].wait()
     local[1].wait()
     for k in range(1, NY):
         arrive(b_slot(0, pair(y, k), 1), B_LINE[k])
-    for s in (1, -1):
-        send(b_slot(0, 0, NY), b_slot(0, 0, NY), B_NEAR[s], dev(dx=s))
-    send(b_slot(0, 0, NY), b_slot(0, 0, NY), B_CORE[0], dev(flip_core=1))
-    arrive(a_slot(0, 1), A_PARTNER)
-    a_send(1, 1, 1)
-    a_send(-1, 1, 1)
-    a_arrive(1, 0, 2)
-    a_arrive(-1, 0, 2)
-    for s in (1, -1):
-        arrive(b_slot(-s, 0, NY), B_NEAR[s])
-        half = b_slot(-s, 0 if s == 1 else NY // 2, NY // 2)
-        send(half, half, B_FAR[s], dev(dx=s))
-        send(b_slot(-s, 0, NY), b_slot(-s, 0, NY), B_CORE[-s], dev(flip_core=1))
-    a_arrive(1, 1, 1)
-    a_arrive(-1, 1, 1)
-    a_arrive(1, 0, 3)
-    a_arrive(-1, 0, 3)
-    for s in (1, -1):
-        half = b_slot(2, 0 if s == 1 else NY // 2, NY // 2)
-        arrive(half, B_FAR[s])
-        send(half, half, B_CORE[2, s], dev(flip_core=1))
-    a_arrive(1, 1, 2)
-    a_arrive(-1, 1, 2)
-    for dx in (0, 1, -1):
-        arrive(b_slot(dx, 0, NY, 1), B_CORE[dx])
-    for s in (1, -1):
-        arrive(b_slot(2, 0 if s == 1 else NY // 2, NY // 2, 1), B_CORE[2, s])
+    b_group = b_slot(0, 0, NY)
+    b_near = {d: message(b_group, b_group, B_X[d], dev(dx=d)) for d in X_STEPS}
+    for d, c in b_near.items():
+        @pl.when(x_later(d))
+        def _():
+            told(B_X[d if 2 * d == NX else -d])
+
+        c.start()
+
+    @pl.when(core == 1)
+    def _():
+        told(B_CORE[0])
+
+    b_shared = [message(b_group, b_group, B_CORE[0], dev(flip_core=1))]
+    b_shared[0].start()
+
+    @pl.when(h == 0)
+    def _():
+        arrive(a_slot(z, 1), A_PARTNER)
+        for t in range(NZ - 1):
+            @pl.when(t < z)
+            def _():
+                a_message(1, t).start()
+
+    for t in range(1, NZ):
+        @pl.when(t > z)
+        def _():
+            told(A_Z + (z - t + NZ) % NZ)
+            a_message(0, t).start()
+
+            @pl.when(h == 0)
+            def _():
+                a_message(1, t).start()
+
+    @pl.when(h == 1)
+    def _():
+        arrive(a_slot(z, 1), A_PARTNER)
+        for t in range(NZ):
+            @pl.when(t != z)
+            def _():
+                a_message(1, t).start()
+
+    for d in X_STEPS[::-1]:
+        group_b = b_slot(-d, 0, NY)
+        arrive(group_b, B_X[d])
+        b_shared.append(message(group_b, group_b, B_CORE[d], dev(flip_core=1)))
+        b_shared[-1].start()
+    for d in (0, *X_STEPS[::-1]):
+        arrive(b_slot(-d, 0, NY, 1), B_CORE[d])
 
     def split(v):
         high = v.astype(jnp.bfloat16)
@@ -172,16 +247,12 @@
                     b_cat[l, pl.ds(to, rows_owned), 128:256] = high
                     b_cat[l, pl.ds(to, rows_owned), 256:384] = low
 
-    a_arrive(1, 1, 3)
-    a_arrive(-1, 1, 3)
-    a_arrive(1, 0, 4)
     local[4].wait()
     local[5].wait()
 
     group = 2 * NH * cols_owned
 
-    def merge(dj):
-        j = (z // 2 + dj + NZ // 2) % (NZ // 2)
+    def merge(j):
         first = pl.multiple_of(j * group, 16)
         for l, out in ((0, oh_ref), (1, of_ref)):
             high, low = split(a_all[pl.ds(first * 2 + l, group, stride=2), :])
@@ -192,11 +263,28 @@
             at = (pl.ds(first, group), slice(None))
             out[at] = (out[at].astype(jnp.float32) + MERGE_SCALE * update).astype(out.dtype)
 
-    merge(0)
-    merge(1)
-    merge(-1)
-    a_arrive(-1, 1, 4)
-    merge(2)
+    for t in range(NZ):
+        @pl.when(t != z)
+        def _():
+            a_arrive(0, t)
+
+    def partner_pair(dj):
+        j = (z // 2 + dj + NZ // 2) % (NZ // 2)
+        for t in (2 * j, 2 * j + 1):
+            @pl.when(t != z)
+            def _():
+                a_arrive(1, t)
+        merge(j)
+
+    for dj in (0, 1, -1, 2):
+        partner_pair(dj)
+
+    sent = [partner, *b_line.values(), *b_near.values(), *b_shared]
+    for t in range(NZ):
+        @pl.when(t != z)
+        def _():
+            for o in range(NH):
+                a_message(o, t).wait_send()
     for c in sent:
         c.wait_send()
 
@@ -241,6 +329,7 @@
             pltpu.SemaphoreType.DMA((MESSAGES,)),
             pltpu.SemaphoreType.DMA((MESSAGES,)),
             pltpu.SemaphoreType.DMA((8,)),
+            pltpu.SemaphoreType.REGULAR((B_X[X_STEPS[-1]] + 2,)),
         ],
         compiler_params=pltpu.CompilerParams(
             collective_id=0, has_side_effects=True, vmem_limit_bytes=32 * 1024 * 1024

time: 34.4 us -> 27.7 us (0.81)
  the two profiles are of different devices: /device:TPU:16 before, /device:TPU:62 now
where the time goes in v2:
time: 27.7 us; the launch traced here: 27.5 us
  Pallas kernels  26.9 us (97%)
  between operations  0.64 us (2%)
    pallas_call x1, Pallas kernels, per_device(): pl.pallas_call(gather_merge, name='gather_merge', out_shape=[pltpu.VMEM(s...  25.8 us
    pallas_call x1, Pallas kernels, per_device(): pl.pallas_call(deliver, name='deliver', out_shape=[jax.ShapeDtypeStruct(s...  1.12 us

profile of v2, /device:TPU:62, one launch (start us, length us, event | category | flops | bytes accessed | tf_op | source)
XLA Modules:
  0.0 27.5 jit_solution(15334785765361464813)
XLA Ops:
  0.6 25.8 %gather_merge.1 = (bf16[448,512]{1,0:T(8,128)(2,1)S(1)}, f32[448,512]{1,0:T(8,128)S(1)}, f32[2,32,128]{2,1,0:T(8,128)S(1)}, f32[2,56,128]{2,1,0:T(8,128)S(1)}) custom-call(bf16[448,512]{1,0:T(8,128)(2,1)} %bitcast.17, f32[448,512]{1,0:T(8,128)} %bitcast.16, f32[32,128]{1,0:T(8,128)} %bitcast.21, f32[56,128]{1,0:T(8,128)} %bitcast.20, ...), custom_call_target="tpu_custom_call" | custom-call | tf_op jit(solution)/shard_map/gather_merge/pallas_call | solution.py:317
  26.4 1.1 %deliver.1 = (bf16[448,512]{1,0:T(8,128)(2,1)}, f32[448,512]{1,0:T(8,128)}, f32[2,32,128]{2,1,0:T(8,128)}, f32[2,56,128]{2,1,0:T(8,128)}) custom-call(bf16[448,512]{1,0:T(8,128)(2,1)S(1)} %get-tuple-element.12.refs_0_, f32[448,512]{1,0:T(8,128)S(1)} %get-tuple-element.13.refs_1_, f32[2,32,128]{2,1,0:T(8,128)S(1)} %get-tuple-element.14.refs_2_, ...), custom_call_target="tpu_custom_call" | custom-call | tf_op jit(solution)/shard_map/deliver/pallas_call | solution.py:342

commit v3 on v2

--- a/solution.py
+++ b/solution.py
@@ -13,6 +13,7 @@
 MESH = pl.DeviceIdType.MESH
 NZ, NH, NY, NX, NC = 8, 2, 4, 4, 2
 X_STEPS = (2, 1, -1)
+FAR = 3
 A_PARTNER = 0
 A_Z = 1
 B_FIRST = A_Z + NH * NZ
@@ -198,11 +199,22 @@
     b_shared = [message(b_group, b_group, B_CORE[0], dev(flip_core=1))]
     b_shared[0].start()
 
+    def far(t):
+        steps = (t - z + NZ) % NZ
+        return jnp.logical_and(steps >= FAR, steps <= NZ - FAR)
+
+    def close(t):
+        return jnp.logical_and(t != z, jnp.logical_not(far(t)))
+
+    def a_crossing(t):
+        slot = a_slot(t, 0)
+        return message(slot, slot, A_Z + NZ + (z - t + NZ) % NZ, dev(flip_h=1))
+
     @pl.when(h == 0)
     def _():
         arrive(a_slot(z, 1), A_PARTNER)
         for t in range(NZ - 1):
-            @pl.when(t < z)
+            @pl.when(jnp.logical_and(t < z, close(t)))
             def _():
                 a_message(1, t).start()
 
@@ -212,7 +224,7 @@
             told(A_Z + (z - t + NZ) % NZ)
             a_message(0, t).start()
 
-            @pl.when(h == 0)
+            @pl.when(jnp.logical_and(h == 0, close(t)))
             def _():
                 a_message(1, t).start()
 
@@ -220,15 +232,22 @@
     def _():
         arrive(a_slot(z, 1), A_PARTNER)
         for t in range(NZ):
-            @pl.when(t != z)
+            @pl.when(close(t))
             def _():
                 a_message(1, t).start()
+
+    for t in range(NZ):
+        @pl.when(far(t))
+        def _():
+            a_arrive(0, t)
+            a_crossing(t).start()
 
     for d in X_STEPS[::-1]:
         group_b = b_slot(-d, 0, NY)
         arrive(group_b, B_X[d])
         b_shared.append(message(group_b, group_b, B_CORE[d], dev(flip_core=1)))
         b_shared[-1].start()
+
     for d in (0, *X_STEPS[::-1]):
         arrive(b_slot(-d, 0, NY, 1), B_CORE[d])
 
@@ -264,7 +283,7 @@
             out[at] = (out[at].astype(jnp.float32) + MERGE_SCALE * update).astype(out.dtype)
 
     for t in range(NZ):
-        @pl.when(t != z)
+        @pl.when(close(t))
         def _():
             a_arrive(0, t)
 
@@ -283,8 +302,15 @@
     for t in range(NZ):
         @pl.when(t != z)
         def _():
-            for o in range(NH):
-                a_message(o, t).wait_send()
+            a_message(0, t).wait_send()
+
+        @pl.when(close(t))
+        def _():
+            a_message(1, t).wait_send()
+
+        @pl.when(far(t))
+        def _():
+            a_crossing(t).wait_send()
     for c in sent:
         c.wait_send()
 

time: 27.7 us -> 26.3 us (0.949)
  the two profiles are of different devices: /device:TPU:62 before, /device:TPU:50 now
where the time goes in v3:
time: 26.3 us; the launch traced here: 26.2 us
  Pallas kernels  25.6 us (97%)
  between operations  0.64 us (2%)
    pallas_call x1, Pallas kernels, per_device(): pl.pallas_call(gather_merge, name='gather_merge', out_shape=[pltpu.VMEM(s...  24.4 us
    pallas_call x1, Pallas kernels, per_device(): pl.pallas_call(deliver, name='deliver', out_shape=[jax.ShapeDtypeStruct(s...  1.12 us

profile of v3, /device:TPU:50, one launch (start us, length us, event | category | flops | bytes accessed | tf_op | source)
XLA Modules:
  0.0 26.2 jit_solution(14069379044493345355)
XLA Ops:
  0.6 24.4 %gather_merge.1 = (bf16[448,512]{1,0:T(8,128)(2,1)S(1)}, f32[448,512]{1,0:T(8,128)S(1)}, f32[2,32,128]{2,1,0:T(8,128)S(1)}, f32[2,56,128]{2,1,0:T(8,128)S(1)}) custom-call(bf16[448,512]{1,0:T(8,128)(2,1)} %bitcast.17, f32[448,512]{1,0:T(8,128)} %bitcast.16, f32[32,128]{1,0:T(8,128)} %bitcast.21, f32[56,128]{1,0:T(8,128)} %bitcast.20, ...), custom_call_target="tpu_custom_call" | custom-call | tf_op jit(solution)/shard_map/gather_merge/pallas_call | solution.py:343
  25.1 1.1 %deliver.1 = (bf16[448,512]{1,0:T(8,128)(2,1)}, f32[448,512]{1,0:T(8,128)}, f32[2,32,128]{2,1,0:T(8,128)}, f32[2,56,128]{2,1,0:T(8,128)}) custom-call(bf16[448,512]{1,0:T(8,128)(2,1)S(1)} %get-tuple-element.12.refs_0_, f32[448,512]{1,0:T(8,128)S(1)} %get-tuple-element.13.refs_1_, f32[2,32,128]{2,1,0:T(8,128)S(1)} %get-tuple-element.14.refs_2_, ...), custom_call_target="tpu_custom_call" | custom-call | tf_op jit(solution)/shard_map/deliver/pallas_call | solution.py:368

commit v4 on v3

--- a/solution.py
+++ b/solution.py
@@ -23,10 +23,24 @@
 MESSAGES = B_FIRST + NY + 2 * len(X_STEPS) + 1
 
 
+def split(v):
+    high = v.astype(jnp.bfloat16)
+    return high, (v - high.astype(jnp.float32)).astype(jnp.bfloat16)
+
+
+def merge(weight, a_rows, b_split):
+    high, low = split(a_rows)
+    update = lax.dot_general(
+        jnp.concatenate([high, low, high], axis=1), b_split,
+        (((1,), (1,)), ((), ())), preferred_element_type=jnp.float32,
+    )
+    return (weight.astype(jnp.float32) + MERGE_SCALE * update).astype(weight.dtype)
+
+
 def gather_merge(
     wh_ref, wf_ref, b_ref, a_ref, mb_ref, ma_ref, rr_ref, rc_ref,
-    oh_ref, of_ref, ob_ref, oa_ref,
-    a_all, b_all, b_cat, row_flags, col_flags, send_sem, recv_sem, local_sem, ready_sem,
+    oh_ref, of_ref, ob_ref, oa_ref, b_cat, a_last,
+    a_all, b_all, row_flags, col_flags, send_sem, recv_sem, local_sem, ready_sem,
 ):
     row, col = lax.axis_index("row"), lax.axis_index("col")
     z, h = row // NH, row % NH
@@ -251,10 +265,6 @@
     for d in (0, *X_STEPS[::-1]):
         arrive(b_slot(-d, 0, NY, 1), B_CORE[d])
 
-    def split(v):
-        high = v.astype(jnp.bfloat16)
-        return high, (v - high.astype(jnp.float32)).astype(jnp.bfloat16)
-
     for by in range(NY):
         for bx in range(NX):
             for bc in range(NC):
@@ -270,33 +280,26 @@
     local[5].wait()
 
     group = 2 * NH * cols_owned
-
-    def merge(j):
-        first = pl.multiple_of(j * group, 16)
-        for l, out in ((0, oh_ref), (1, of_ref)):
-            high, low = split(a_all[pl.ds(first * 2 + l, group, stride=2), :])
-            update = lax.dot_general(
-                jnp.concatenate([high, low, high], axis=1), b_cat[l],
-                (((1,), (1,)), ((), ())), preferred_element_type=jnp.float32,
-            )
-            at = (pl.ds(first, group), slice(None))
-            out[at] = (out[at].astype(jnp.float32) + MERGE_SCALE * update).astype(out.dtype)
+    last = NZ // 2 - 1
 
     for t in range(NZ):
         @pl.when(close(t))
         def _():
             a_arrive(0, t)
 
-    def partner_pair(dj):
-        j = (z // 2 + dj + NZ // 2) % (NZ // 2)
+    for j in range(NZ // 2):
         for t in (2 * j, 2 * j + 1):
             @pl.when(t != z)
             def _():
                 a_arrive(1, t)
-        merge(j)
-
-    for dj in (0, 1, -1, 2):
-        partner_pair(dj)
+
+        rows = pl.ds(j * group, group)
+        for l, out in enumerate((oh_ref, of_ref)):
+            a_rows_l = a_all[pl.ds(j * group * LAYERS + l, group, stride=LAYERS), :]
+            if j < last:
+                out[rows, :] = merge(out[rows, :], a_rows_l, b_cat[l])
+            else:
+                a_last[l] = a_rows_l
 
     sent = [partner, *b_line.values(), *b_near.values(), *b_shared]
     for t in range(NZ):
@@ -315,14 +318,25 @@
         c.wait_send()
 
 
-def deliver(*refs):
-    sems = refs[-1]
-    half = (len(refs) - 1) // 2
+def deliver(
+    wh_ref, wf_ref, mb_ref, ma_ref, b_cat, a_last,
+    oh_ref, of_ref, ob_ref, oa_ref, last_h, last_f, sems,
+):
+    group = a_last.shape[1]
+    done = wh_ref.shape[0] - group
+    first, rest = pl.ds(0, done), pl.ds(done, group)
     copies = [
-        pltpu.make_async_copy(refs[i], refs[half + i], sems.at[i]) for i in range(half)
+        pltpu.make_async_copy(wf_ref.at[first], of_ref.at[first], sems.at[0]),
+        pltpu.make_async_copy(wh_ref.at[first], oh_ref.at[first], sems.at[1]),
+        pltpu.make_async_copy(mb_ref, ob_ref, sems.at[2]),
+        pltpu.make_async_copy(ma_ref, oa_ref, sems.at[3]),
     ]
     for c in copies:
         c.start()
+    for l, (weight, part, out) in enumerate(((wh_ref, last_h, oh_ref), (wf_ref, last_f, of_ref))):
+        part[...] = merge(weight[rest, :], a_last[l], b_cat[l])
+        copies.append(pltpu.make_async_copy(part, out.at[rest], sems.at[4 + l]))
+        copies[-1].start()
     for c in copies:
         c.wait()
 
@@ -338,18 +352,21 @@
     mb = moments_b.reshape(layers, 2 * rows_owned, rank)
     ma = moments_a.transpose(0, 3, 1, 2).reshape(layers, cols_owned * 2, rank)
     shapes = [wh, wf, mb, ma]
+    group = 2 * NH * cols_owned
     hbm = pl.BlockSpec(memory_space=pl.ANY)
     vmem = pl.BlockSpec(memory_space=pltpu.VMEM)
     merged = pl.pallas_call(
         gather_merge,
         name="gather_merge",
-        out_shape=[pltpu.VMEM(s.shape, s.dtype) for s in shapes],
+        out_shape=[pltpu.VMEM(s.shape, s.dtype) for s in shapes] + [
+            pltpu.VMEM((layers, NY * NX * NC * rows_owned, 3 * rank), jnp.bfloat16),
+            pltpu.VMEM((layers, group, rank), jnp.float32),
+        ],
         in_specs=[hbm] * 8,
-        out_specs=[vmem] * 4,
+        out_specs=[vmem] * 6,
         scratch_shapes=[
             pltpu.VMEM((NZ * NH * a.shape[0], rank), jnp.float32),
             pltpu.VMEM((NY * NX * NC * b.shape[0], rank), jnp.float32),
-            pltpu.VMEM((layers, NY * NX * NC * rows_owned, 3 * rank), jnp.bfloat16),
             pltpu.SMEM(reset_rows.shape, jnp.int32),
             pltpu.SMEM(reset_cols.shape, jnp.int32),
             pltpu.SemaphoreType.DMA((MESSAGES,)),
@@ -369,9 +386,14 @@
         deliver,
         name="deliver",
         out_shape=[jax.ShapeDtypeStruct(s.shape, s.dtype) for s in shapes],
-        in_specs=[vmem] * 4,
+        in_specs=[vmem] * 6,
         out_specs=[hbm] * 4,
-        scratch_shapes=[pltpu.SemaphoreType.DMA((4,))],
+        scratch_shapes=[
+            pltpu.VMEM((group, wh.shape[1]), wh.dtype),
+            pltpu.VMEM((group, wf.shape[1]), wf.dtype),
+            pltpu.SemaphoreType.DMA((6,)),
+        ],
+        compiler_params=pltpu.CompilerParams(vmem_limit_bytes=32 * 1024 * 1024),
     )(*merged)
     oa = oa.reshape(layers, cols_owned, 2, rank).transpose(0, 2, 3, 1)
     return oh.T, of.T, ob.reshape(moments_b.shape), oa

time: 26.3 us -> 25.9 us (0.985)
  the two profiles are of different devices: /device:TPU:50 before, /device:TPU:134 now
where the time goes in v4:
time: 25.9 us; the launch traced here: 25.7 us
  Pallas kernels  25.1 us (97%)
  between operations  0.64 us (2%)
    pallas_call x1, Pallas kernels, per_device(): pl.pallas_call(gather_merge, name='gather_merge', out_shape=[pltpu.VMEM(s...  23.9 us
    pallas_call x1, Pallas kernels, per_device(): pl.pallas_call(deliver, name='deliver', out_shape=[jax.ShapeDtypeStruct(s...  1.16 us

profile of v4, /device:TPU:134, one launch (start us, length us, event | category | flops | bytes accessed | tf_op | source)
XLA Modules:
  0.0 25.7 jit_solution(6648045580886905018)
XLA Ops:
  0.6 23.9 %gather_merge.1 = (bf16[448,512]{1,0:T(8,128)(2,1)S(1)}, f32[448,512]{1,0:T(8,128)S(1)}, f32[2,32,128]{2,1,0:T(8,128)S(1)}, f32[2,56,128]{2,1,0:T(8,128)S(1)}, b...) custom-call(bf16[448,512]{1,0:T(8,128)(2,1)} %bitcast.17, f32[448,512]{1,0:T(8,128)} %bitcast.16, ...), custom_call_target="tpu_custom_call" | custom-call | tf_op jit(solution)/shard_map/gather_merge/pallas_call | solution.py:358
  24.6 1.2 %deliver.1 = (bf16[448,512]{1,0:T(8,128)(2,1)}, f32[448,512]{1,0:T(8,128)}, f32[2,32,128]{2,1,0:T(8,128)}, f32[2,56,128]{2,1,0:T(8,128)}) custom-call(bf16[448,512]{1,0:T(8,128)(2,1)S(1)} %get-tuple-element.14.wh_ref, f32[448,512]{1,0:T(8,128)S(1)} %get-tuple-element.15.wf_ref, f32[2,32,128]{2,1,0:T(8,128)S(1)} %get-tuple-element.16.mb_ref, ...), custom_call_target="tpu_custom_call" | custom-call | tf_op jit(solution)/shard_map/deliver/pallas_call | solution.py:385

commit v5 on v4

--- a/solution.py
+++ b/solution.py
@@ -13,7 +13,6 @@
 MESH = pl.DeviceIdType.MESH
 NZ, NH, NY, NX, NC = 8, 2, 4, 4, 2
 X_STEPS = (2, 1, -1)
-FAR = 3
 A_PARTNER = 0
 A_Z = 1
 B_FIRST = A_Z + NH * NZ
@@ -213,12 +212,14 @@
     b_shared = [message(b_group, b_group, B_CORE[0], dev(flip_core=1))]
     b_shared[0].start()
 
-    def far(t):
-        steps = (t - z + NZ) % NZ
-        return jnp.logical_and(steps >= FAR, steps <= NZ - FAR)
-
-    def close(t):
-        return jnp.logical_and(t != z, jnp.logical_not(far(t)))
+    def crosses(origin, to):
+        steps = (origin - to + NZ) % NZ
+        return jnp.logical_or(
+            jnp.logical_or(steps == 5, steps == 4), jnp.logical_and(steps == 3, core == 1)
+        )
+
+    def sends_to(t):
+        return jnp.logical_and(t != z, jnp.logical_not(crosses(z, t)))
 
     def a_crossing(t):
         slot = a_slot(t, 0)
@@ -228,7 +229,7 @@
     def _():
         arrive(a_slot(z, 1), A_PARTNER)
         for t in range(NZ - 1):
-            @pl.when(jnp.logical_and(t < z, close(t)))
+            @pl.when(jnp.logical_and(t < z, sends_to(t)))
             def _():
                 a_message(1, t).start()
 
@@ -238,7 +239,7 @@
             told(A_Z + (z - t + NZ) % NZ)
             a_message(0, t).start()
 
-            @pl.when(jnp.logical_and(h == 0, close(t)))
+            @pl.when(jnp.logical_and(h == 0, sends_to(t)))
             def _():
                 a_message(1, t).start()
 
@@ -246,12 +247,12 @@
     def _():
         arrive(a_slot(z, 1), A_PARTNER)
         for t in range(NZ):
-            @pl.when(close(t))
+            @pl.when(sends_to(t))
             def _():
                 a_message(1, t).start()
 
     for t in range(NZ):
-        @pl.when(far(t))
+        @pl.when(crosses(t, z))
         def _():
             a_arrive(0, t)
             a_crossing(t).start()
@@ -283,7 +284,7 @@
     last = NZ // 2 - 1
 
     for t in range(NZ):
-        @pl.when(close(t))
+        @pl.when(jnp.logical_and(t != z, jnp.logical_not(crosses(t, z))))
         def _():
             a_arrive(0, t)
 
@@ -307,11 +308,11 @@
         def _():
             a_message(0, t).wait_send()
 
-        @pl.when(close(t))
+        @pl.when(sends_to(t))
         def _():
             a_message(1, t).wait_send()
 
-        @pl.when(far(t))
+        @pl.when(crosses(t, z))
         def _():
             a_crossing(t).wait_send()
     for c in sent:

time: 25.9 us -> 25.8 us (level)
  no operation moved by 1% of the time
where the time goes in v5:
time: 25.8 us; the launch traced here: 25.6 us
  Pallas kernels  25 us (97%)
  between operations  0.64 us (2%)
    pallas_call x1, Pallas kernels, per_device(): pl.pallas_call(gather_merge, name='gather_merge', out_shape=[pltpu.VMEM(s...  23.8 us
    pallas_call x1, Pallas kernels, per_device(): pl.pallas_call(deliver, name='deliver', out_shape=[jax.ShapeDtypeStruct(s...  1.16 us

profile of v5, /device:TPU:134, one launch (start us, length us, event | category | flops | bytes accessed | tf_op | source)
XLA Modules:
  0.0 25.6 jit_solution(14570008480680581628)
XLA Ops:
  0.6 23.8 %gather_merge.1 = (bf16[448,512]{1,0:T(8,128)(2,1)S(1)}, f32[448,512]{1,0:T(8,128)S(1)}, f32[2,32,128]{2,1,0:T(8,128)S(1)}, f32[2,56,128]{2,1,0:T(8,128)S(1)}, b...) custom-call(bf16[448,512]{1,0:T(8,128)(2,1)} %bitcast.17, f32[448,512]{1,0:T(8,128)} %bitcast.16, ...), custom_call_target="tpu_custom_call" | custom-call | tf_op jit(solution)/shard_map/gather_merge/pallas_call | solution.py:359
  24.5 1.2 %deliver.1 = (bf16[448,512]{1,0:T(8,128)(2,1)}, f32[448,512]{1,0:T(8,128)}, f32[2,32,128]{2,1,0:T(8,128)}, f32[2,56,128]{2,1,0:T(8,128)}) custom-call(bf16[448,512]{1,0:T(8,128)(2,1)S(1)} %get-tuple-element.14.wh_ref, f32[448,512]{1,0:T(8,128)S(1)} %get-tuple-element.15.wf_ref, f32[2,32,128]{2,1,0:T(8,128)S(1)} %get-tuple-element.16.mb_ref, ...), custom_call_target="tpu_custom_call" | custom-call | tf_op jit(solution)/shard_map/deliver/pallas_call | solution.py:386

commit v6 on v5

--- a/solution.py
+++ b/solution.py
@@ -225,31 +225,17 @@
         slot = a_slot(t, 0)
         return message(slot, slot, A_Z + NZ + (z - t + NZ) % NZ, dev(flip_h=1))
 
-    @pl.when(h == 0)
-    def _():
-        arrive(a_slot(z, 1), A_PARTNER)
-        for t in range(NZ - 1):
-            @pl.when(jnp.logical_and(t < z, sends_to(t)))
-            def _():
-                a_message(1, t).start()
-
     for t in range(1, NZ):
         @pl.when(t > z)
         def _():
             told(A_Z + (z - t + NZ) % NZ)
             a_message(0, t).start()
 
-            @pl.when(jnp.logical_and(h == 0, sends_to(t)))
-            def _():
-                a_message(1, t).start()
-
-    @pl.when(h == 1)
-    def _():
-        arrive(a_slot(z, 1), A_PARTNER)
-        for t in range(NZ):
-            @pl.when(sends_to(t))
-            def _():
-                a_message(1, t).start()
+    arrive(a_slot(z, 1), A_PARTNER)
+    for t in range(NZ):
+        @pl.when(sends_to(t))
+        def _():
+            a_message(1, t).start()
 
     for t in range(NZ):
         @pl.when(crosses(t, z))

time: 25.8 us -> 25.9 us (level)
  the two profiles are of different devices: /device:TPU:134 before, /device:TPU:48 now
where the time goes in v6:
time: 25.9 us; the launch traced here: 25.8 us
  Pallas kernels  25.2 us (97%)
  between operations  0.64 us (2%)
    pallas_call x1, Pallas kernels, per_device(): pl.pallas_call(gather_merge, name='gather_merge', out_shape=[pltpu.VMEM(s...  24 us
    pallas_call x1, Pallas kernels, per_device(): pl.pallas_call(deliver, name='deliver', out_shape=[jax.ShapeDtypeStruct(s...  1.16 us

profile of v6, /device:TPU:48, one launch (start us, length us, event | category | flops | bytes accessed | tf_op | source)
XLA Modules:
  0.0 25.8 jit_solution(11593486004282929272)
XLA Ops:
  0.6 24.0 %gather_merge.1 = (bf16[448,512]{1,0:T(8,128)(2,1)S(1)}, f32[448,512]{1,0:T(8,128)S(1)}, f32[2,32,128]{2,1,0:T(8,128)S(1)}, f32[2,56,128]{2,1,0:T(8,128)S(1)}, b...) custom-call(bf16[448,512]{1,0:T(8,128)(2,1)} %bitcast.17, f32[448,512]{1,0:T(8,128)} %bitcast.16, ...), custom_call_target="tpu_custom_call" | custom-call | tf_op jit(solution)/shard_map/gather_merge/pallas_call | solution.py:345
  24.6 1.2 %deliver.1 = (bf16[448,512]{1,0:T(8,128)(2,1)}, f32[448,512]{1,0:T(8,128)}, f32[2,32,128]{2,1,0:T(8,128)}, f32[2,56,128]{2,1,0:T(8,128)}) custom-call(bf16[448,512]{1,0:T(8,128)(2,1)S(1)} %get-tuple-element.14.wh_ref, f32[448,512]{1,0:T(8,128)S(1)} %get-tuple-element.15.wf_ref, f32[2,32,128]{2,1,0:T(8,128)S(1)} %get-tuple-element.16.mb_ref, ...), custom_call_target="tpu_custom_call" | custom-call | tf_op jit(solution)/shard_map/deliver/pallas_call | solution.py:372
